TPU v7x, 512 devices: a whole 4x8x8 slice. The times are simulated.
512 devices in a mesh: group: 16 (over x_lo, z), dev: 32 (over x_hi, y, core).
Axes of the slice: x: 4 (x_hi: 2, x_lo: 2; x = x_hi * 2 + x_lo), y: 8, z: 8, core: 2. Of those that a mesh axis runs over, the one named last changes fastest.
Arguments:
- patches: bfloat16 [16, 32, 256, 1152], P('group', 'dev'), may hold values from -6 to 6
- norm_gain: float32 [1152], replicated, may hold values from 0.1 to 1.9
- kv_weight: bfloat16 [4096, 1152], P(('group', 'dev')), may hold values from -0.1875 to 0.1875
- latent_q: bfloat16 [64, 2048], replicated
- clip_frames: int32 [16, 32], P('group', 'dev'), may hold values from 1 to 8, as said below
- row_owner: int32 [16, 32, 256], P('group', 'dev'), may hold values from 0 to 31, as said below
- row_slot: int32 [16, 32, 256], P('group', 'dev'), may hold values from 0 to 15, as said below
- slot_pos: int32 [16, 32, 512], P('group', 'dev'), may hold values from 0 to 512, as said below
- latent_blocks: int32 [16, 32, 64, 2], P('group', 'dev'), may hold values from -1 to 3, as said below
Outputs:
- latent_out: bfloat16 [2048, 32768], P('dev', 'group')
Inputs may be any that keep to these rules, and one draw needn't show every extreme that they name: `clip_frames`: A group's clips hold 4 * 32 frames together; every group has a clip of 8 frames and one of 2 frames or fewer. `row_owner`: A device holds exactly f * 2 rows of each clip of its group that has f frames. `row_slot`: the rows that one device holds for one clip carry the slots 0, 1, and so on, each once. `slot_pos`: for a clip of f frames the entries s * 16 + k, with k below the number of rows of that clip on device s, name the positions 0 to f * 64 - 1 each once; every other entry is 512. `latent_blocks`: for a clip of b = ceil(f / 2) blocks, entry 0 of latent i is block i * b // 64; entry 1 is a block beside it, or -1 where b is 1.
All inputs are finite; a program needn't handle non-finite values.
Results may differ from a plain program's by a relative error of at most 0.0055.
The roundings to bfloat16 on the way count: a program that leaves them out, or rounds other values in their place, can miss the bound.
Values may be sent and summed in bfloat16 or wider, within the bound.
A program may use at most 64 MiB of HBM per device.

v0:
```python
import jax
import jax.numpy as jnp
from jax import lax
from jax.sharding import PartitionSpec as P

HD = 128
LAT = 64
FR_ROWS = 64


def rms_rows(patch_rows, norm_gain):
    widened = patch_rows.astype(jnp.float32)
    inverse_rms = lax.rsqrt(jnp.mean(widened * widened, axis=-1, keepdims=True) + 1e-06)
    return (widened * inverse_rms * norm_gain).astype(jnp.bfloat16)


def product_rows(input_rows, weight_piece):
    return lax.dot_general(
        input_rows, weight_piece, (((1,), (1,)), ((), ())), preferred_element_type=jnp.float32
    )


def project(input_rows, kv_weight, live_rows):
    block_rows = 2 * FR_ROWS
    block_count = input_rows.shape[0] // block_rows
    weight_piece = lax.all_gather(kv_weight, ("group", "dev"), axis=0, tiled=True)
    outputs = []
    for block in range(block_count):
        rows_here = input_rows[block * block_rows : (block + 1) * block_rows]
        empty = jnp.zeros((block_rows, weight_piece.shape[0]), jnp.float32)
        outputs.append(
            lax.cond(
                block * block_rows < live_rows,
                lambda: product_rows(rows_here, weight_piece),
                lambda: empty,
            )
        )
    projected = jnp.concatenate(outputs, axis=0)
    return projected.astype(jnp.bfloat16)


def attend(keyval, frames, listed, latent_q):
    capacity = keyval.shape[0]
    kv_width = keyval.shape[1] // 2
    head_count = kv_width // HD
    key_part = keyval[:, :kv_width].reshape(capacity, head_count, HD)
    value_part = keyval[:, kv_width:].reshape(capacity, head_count, HD)
    queries = latent_q.reshape(LAT, head_count, HD)
    scores = jnp.einsum(
        "ihd,jhd->hij", queries, key_part, preferred_element_type=jnp.float32
    ) * HD ** (-0.5)
    position = jnp.arange(capacity, dtype=jnp.int32)
    block_id = position // (2 * FR_ROWS)
    allowed = ((block_id[None, :] == listed[:, 0:1]) | (block_id[None, :] == listed[:, 1:2])) & (
        position[None, :] < frames * FR_ROWS
    )
    scores = jnp.where(allowed[None, :, :], scores, jnp.float32(-1e30))
    row_max = jnp.max(scores, axis=-1, keepdims=True)
    raised = jnp.exp(scores - row_max)
    row_sum = jnp.sum(raised, axis=-1, keepdims=True)
    attn_weights = (raised / row_sum).astype(jnp.bfloat16)
    blended = jnp.einsum(
        "hij,jhd->hdi", attn_weights, value_part, preferred_element_type=jnp.float32
    )
    return blended.astype(jnp.bfloat16).reshape(kv_width, LAT)


def per_device(
    patches,
    norm_gain,
    kv_weight,
    latent_q,
    clip_frames,
    row_owner,
    row_slot,
    slot_pos,
    latent_blocks,
):
    dev_count = lax.axis_size("dev")
    normed = rms_rows(patches[0, 0], norm_gain)
    places = slot_pos[0, 0]
    capacity = places.shape[0]
    slot_count = capacity // dev_count
    target = row_owner[0, 0] * slot_count + row_slot[0, 0]
    frames = clip_frames[0, 0]
    outbox = jnp.zeros((capacity, normed.shape[1]), jnp.bfloat16).at[target].set(normed)
    received = lax.all_to_all(
        outbox.reshape(dev_count, slot_count, normed.shape[1]),
        "dev",
        split_axis=0,
        concat_axis=0,
        tiled=True,
    )
    timeline = (
        jnp.zeros_like(outbox)
        .at[places]
        .set(received.reshape(capacity, normed.shape[1]), mode="drop")
    )
    keyval = project(timeline, kv_weight, frames * FR_ROWS)
    blended = attend(keyval, frames, latent_blocks[0, 0], latent_q)
    return lax.all_to_all(blended, "dev", split_axis=0, concat_axis=1, tiled=True)


def solution(mesh):
    return jax.shard_map(
        per_device,
        mesh=mesh,
        in_specs=(
            P("group", "dev", None, None),
            P(),
            P(("group", "dev"), None),
            P(),
            P("group", "dev"),
            P("group", "dev", None),
            P("group", "dev", None),
            P("group", "dev", None),
            P("group", "dev", None, None),
        ),
        out_specs=P("dev", "group"),
        check_vma=False,
    )
```

profile of v0, /device:TPU:7, one launch (start us, length us, event | category | flops | bytes accessed | tf_op | source)
XLA Modules:
  0.0 906.9 jit_solution(12294368740215103621)
XLA Ops:
  6.5 0.7 all-gather.2.cloned.1.call-update
  7.3 1.3 fusion.10
  8.6 0.7 compare_select_fusion.1
  9.3 3.3 scatter_custom_fusion
  12.6 10.5 %all-to-all-start = ((bf16[32,16,1152]{2,1,0:T(8,128)(2,1)}), bf16[32,16,1152]{2,1,0:T(8,128)(2,1)S(1)}, u32[]{:S(2)}, u32[]{:S(2)}) async-start(bf16[32,16,1152]{2,1,0:T(8,128)(2,1)} %bitcast.7), calls=%async_computation | async-start | bytes 2359296 | tf_op jit(solution)/shard_map/all_to_all | solution.py:87
  23.9 0.7 or_and_fusion
  24.6 29.3 %all-to-all-done = bf16[32,16,1152]{2,1,0:T(8,128)(2,1)S(1)} async-done(((bf16[32,16,1152]{2,1,0:T(8,128)(2,1)}), bf16[32,16,1152]{2,1,0:T(8,128)(2,1)S(1)}, u32[]{:S(2)}, u32[]{:S(2)}) %all-to-all-start) | async-done | bytes 1179680 | tf_op jit(solution)/shard_map/all_to_all | solution.py:87
  53.9 3.1 scatter_custom_fusion.1
  57.0 777.4 %all-gather.2.cloned.1.call-done = bf16[4096,1152]{1,0:T(8,128)(2,1)} async-done(((bf16[8,1152]{1,0:T(8,128)(2,1)}), bf16[4096,1152]{1,0:T(8,128)(2,1)}) %all-gather.2.cloned.1.call-update) | async-done | bytes 9437200 | tf_op jit(solution)/shard_map/all_gather | solution.py:26
  834.4 6.8 conditional.4
  834.4 6.8 fusion
  841.2 0.7 copy.28
  841.9 6.8 conditional.5
  841.9 6.8 fusion.2
  848.7 1.3 copy.29
  850.1 1.3 copy.30
  851.7 1.3 copy.31
  853.0 1.8 pad_maximum_fusion
  854.8 1.6 fusion.37
  856.4 0.4 fusion.24
  857.2 0.7 fusion.38
  857.9 3.5 convolution_convert_fusion
  862.4 36.4 %all_to_all.24 = bf16[32,2,2048]{2,1,0:T(2,128)(2,1)S(1)} all-to-all(bf16[32,2,2048]{2,1,0:T(2,128)(2,1)S(1)} %reshape.211), channel_id=1, replica_groups=mesh['group'=16,'dev'=32] {'dev'}, dimensions={0} | all-to-all | bytes 524288 | tf_op jit(solution)/shard_map/all_to_all | solution.py:101
  899.2 0.9 copy.40
  (25 shorter events, 2.3 us)
Async XLA Ops:
  6.5 849.9 %copy-start = (bf16[64,2048]{1,0:T(8,128)(2,1)S(1)}, bf16[64,2048]{1,0:T(8,128)(2,1)}, u32[]{:S(2)}) copy-start(bf16[64,2048]{1,0:T(8,128)(2,1)} %param.20) | copy-start | bytes 786436
  6.5 827.9 %all-gather.2.cloned.1.call-start = ((), (), s32[]{:S(2)}) async-start(), calls=%async_computation.2 | async-start | bytes 9455616 | tf_op jit(solution)/shard_map/all_gather | solution.py:26
  8.5 15.3 %copy-start.4 = (s32[1,1,64,2]{2,3,1,0:T(2,128)S(1)}, s32[1,1,64,2]{2,3,1,0:T(2,128)}, u32[]{:S(2)}) copy-start(s32[1,1,64,2]{2,3,1,0:T(2,128)} %param.25) | copy-start | bytes 1540
  8.5 15.3 %copy-start.3 = (s32[1,1,512]{2,1,0:T(1,128)S(1)}, s32[1,1,512]{2,1,0:T(1,128)}, u32[]{:S(2)}) copy-start(s32[1,1,512]{2,1,0:T(1,128)} %param.24) | copy-start | bytes 6148
  12.6 41.3 %all-to-all-start = ((bf16[32,16,1152]{2,1,0:T(8,128)(2,1)}), bf16[32,16,1152]{2,1,0:T(8,128)(2,1)S(1)}, u32[]{:S(2)}, u32[]{:S(2)}) async-start(bf16[32,16,1152]{2,1,0:T(8,128)(2,1)} %bitcast.7), calls=%async_computation | async-start | bytes 2359296 | tf_op jit(solution)/shard_map/all_to_all | solution.py:87
  851.7 1.3 copy-start.1
  856.4 0.8 copy-start.2
Sparse Core Ops, SparseCore 0:
  9.6 824.8 all-gather.1
where the time goes:
time: 912 us; the launch traced here: 907 us
  waiting for transfers between devices  807 us (88%)
  blocking collectives  36.4 us (4%)
  matrix products  17.5 us (2%)
  between operations  14.2 us (2%)
  local copies, waits for them, and re-layouts  12.1 us (1%)
  starting transfers between devices  10.5 us (1%)
    all_gather x1, waiting for transfers between devices, project(): lax.all_gather(kv_weight, ('group', 'dev'), axis=0, tiled=True)  777 us
    all_to_all x1, blocking collectives, per_device(): lax.all_to_all(blended, 'dev', split_axis=0, concat_axis=1, tiled=True)  36.4 us
    all_to_all x1, waiting for transfers between devices, per_device(): lax.all_to_all(outbox.reshape(dev_count, slot_count, normed.shape[1]), 'd...  29.3 us
  transfers between devices with their start and end apart: 2, of which 2 were waited for; matrix products, arithmetic and copies ran while one was open for 1% of the time, Pallas kernels for 0%

commit v1 on v0

v1 whole, which is shorter than its diff:
```python
import jax
import jax.numpy as jnp
from jax import lax
from jax.experimental import pallas as pl
from jax.experimental.pallas import tpu as pltpu
from jax.sharding import PartitionSpec as P

HD = 128
LAT = 64
FR_ROWS = 64
V = 1152
COLS_A = 640
COLS_B = 512
CAP = 512
SLOT = 16
NX, NY, NZ = 4, 8, 8
CHIPS = 16
MESH = pl.DeviceIdType.MESH
F32 = jnp.float32
BF16 = jnp.bfloat16


def device_at(x, y, z, core):
    return ((x % 2) * NZ + z, (x // 2) * 2 * NY + y * 2 + core)


def slab_at(x, z):
    return ((x % 2) * NZ + z) * 2 + x // 2


def offsets(n):
    found = [0]
    for step in range(1, n // 2):
        found += [step, -step]
    return found + [n // 2]


def nt_dot(left, right):
    return lax.dot_general(left, right, (((1,), (1,)), ((), ())), preferred_element_type=F32)


def remote(src, dst, send_sem, recv_sem, target):
    return pltpu.make_async_remote_copy(
        src_ref=src,
        dst_ref=dst,
        send_sem=send_sem,
        recv_sem=recv_sem,
        device_id=target,
        device_id_type=MESH,
    )


def kernel(
    patches,
    gain,
    weight,
    queries,
    frames,
    owner,
    slot,
    places,
    listed,
    out,
    part_a,
    part_b,
    rows,
    outbox,
    wide,
    masks,
    packed,
    pair_s,
    pair_r,
    ring_y_s,
    ring_y_r,
    first_s,
    first_r,
    second_s,
    second_r,
    swap_s,
    swap_r,
    send_s,
    send_r,
    hand_s,
    hand_r,
    mask_s,
    mask_r,
    out_s,
    out_r,
):
    group = lax.axis_index("group")
    dev = lax.axis_index("dev")
    x_lo, z = group // NZ, group % NZ
    x_hi, in_line = dev // (2 * NY), dev % (2 * NY)
    y, core = in_line // 2, in_line % 2
    x = x_hi * 2 + x_lo
    chip = dev // 2
    sibling = (group, chip * 2 + 1 - core)

    barrier = pltpu.get_barrier_semaphore()

    def greet(offset, carry):
        pl.semaphore_signal(
            barrier, inc=1, device_id=(group, (dev + offset) % 32), device_id_type=MESH
        )
        return carry

    lax.fori_loop(1, 32, greet, 0)
    for target in (
        device_at(x, y, (z + 1) % NZ, core),
        device_at(x, y, (z + NZ - 1) % NZ, core),
        device_at((x + 1) % NX, y, z, core),
        device_at((x + NX - 1) % NX, y, z, core),
    ):
        pl.semaphore_signal(barrier, inc=1, device_id=target, device_id_type=MESH)
    pl.semaphore_wait(barrier, 35)

    wide[core] = weight[...].astype(F32)
    pair = remote(wide.at[core], wide.at[core], pair_s, pair_r, sibling)
    pair.start()

    position = places[...]
    block_id = position // (2 * FR_ROWS)
    marks = listed[...]
    allowed = ((block_id == marks[:, 0:1]) | (block_id == marks[:, 1:2])) & (
        position < frames[...] * FR_ROWS
    )
    masks[core] = jnp.where(allowed, F32(1.0), F32(0.0))
    mask_copy = remote(masks.at[core], masks.at[core], mask_s, mask_r, sibling)
    mask_copy.start()
    pair.wait_recv()

    chip_rows = pl.ds(pl.multiple_of(y * 16, 16), 16)
    mine = slab_at(x, z)

    def spread(part, low, high):
        both = jnp.concatenate([wide[0, :, low:high], wide[1, :, low:high]], axis=0)
        part[mine, chip_rows, :] = both.astype(BF16)
        for offset in range(1, NY):
            along_y(part, offset).start()

    def along_y(part, offset):
        block = part.at[mine, chip_rows, :]
        return remote(
            block,
            block,
            ring_y_s.at[offset],
            ring_y_r.at[offset],
            device_at(x, (y + offset) % NY, z, core),
        )

    @pl.when(core == 0)
    def _():
        spread(part_a, 0, COLS_A)

    @pl.when(core == 1)
    def _():
        spread(part_b, COLS_A, V)

    widened = patches[...].astype(F32)
    inverse_rms = lax.rsqrt(jnp.sum(widened * widened, axis=-1, keepdims=True) * (1.0 / V) + 1e-06)
    normed = (widened * inverse_rms * gain[...]).astype(BF16)
    target_slot = owner[...] * SLOT + slot[...]
    onehot = (
        lax.broadcasted_iota(jnp.int32, (CAP, target_slot.shape[1]), 0) == target_slot
    ).astype(F32).astype(BF16)
    outbox[...] = (
        jnp.dot(onehot, normed, preferred_element_type=F32).astype(BF16).reshape(CHIPS, 2, SLOT, V)
    )

    own_rows = pl.ds(pl.multiple_of(dev * SLOT, SLOT), SLOT)

    def dispatch(offset):
        there = (chip + offset) % CHIPS
        return remote(
            outbox.at[there],
            rows.at[:, own_rows, :],
            send_s.at[offset],
            send_r.at[offset],
            (group, there * 2 + core),
        )

    def hand_over(offset):
        source = (chip + CHIPS - offset) % CHIPS
        block = rows.at[:, pl.ds(pl.multiple_of((source * 2 + core) * SLOT, SLOT), SLOT), :]
        return remote(block, block, hand_s.at[offset], hand_r.at[offset], sibling)

    def start_dispatch(offset, carry):
        dispatch(offset).start()
        return carry

    lax.fori_loop(1, CHIPS, start_dispatch, 0)
    rows[:, own_rows, :] = outbox[chip]
    hand_over(0).start()

    def gather(part, n1, at1, n2, at2, slab_of, device_of):
        offs = offsets(n1)
        half1, half2 = n1 // 2, n2 // 2

        def first(k, j, way):
            place = (at1 - way * k + n1) % n1
            block = part.at[slab_of(place, at2), pl.ds(j * 64, 64), :]
            index = ((way + 1) // 2 * half1 + k) * 2 + j
            return remote(
                block,
                block,
                first_s.at[index],
                first_r.at[index],
                device_of((at1 + way + n1) % n1, at2),
            )

        def second(k, t, way):
            place = (at2 - way * k + n2) % n2
            block = part.at[slab_of((at1 + offs[t] + n1) % n1, place)]
            index = ((way + 1) // 2 * half2 + k) * n1 + t
            return remote(
                block,
                block,
                second_s.at[index],
                second_r.at[index],
                device_of(at1, (at2 + way + n2) % n2),
            )

        return first, second, half1, half2, offs

    def swap(part, sx, sz):
        index = (sx % 2) * NZ + sz
        block = part.at[slab_at(sx, sz)]
        return remote(block, block, swap_s.at[index], swap_r.at[index], sibling)

    def run_gather(part, n1, at1, n2, at2, slab_of, device_of, xz_of, other):
        first, second, half1, half2, offs = gather(part, n1, at1, n2, at2, slab_of, device_of)

        def landed(t, place2):
            sx, sz = xz_of((at1 + offs[t] + n1) % n1, place2)

            @pl.when(sx // 2 == other)
            def _():
                swap(part, sx, sz).start()

        def complete(t):
            second(0, t, 1).start()
            second(0, t, -1).start()
            landed(t, at2)

        for offset in range(1, NY):
            along_y(part, offset).wait_recv()
        for j in range(2):
            for way in (1, -1):
                first(0, j, way).start()
        complete(0)
        for k in range(1, half1 + 1):
            for way in (-1, 1):
                for j in range(2):
                    last = k == half1
                    if last and j != (1 - way) // 2:
                        continue
                    first(k - 1, j, way).wait_recv()
                    if k < half1 - 1 or (k == half1 - 1 and j == (1 - way) // 2):
                        first(k, j, way).start()
                if k < half1:
                    complete(2 * k if way == 1 else 2 * k - 1)
        complete(n1 - 1)
        for k in range(1, half2 + 1):
            for t in range(n1):
                for way in (1, -1):
                    chosen = t % 2 == (1 - way) // 2
                    if k == half2 and not chosen:
                        continue
                    second(k - 1, t, way).wait_recv()
                    if k < half2 - 1 or (k == half2 - 1 and chosen):
                        second(k, t, way).start()
                    landed(t, (at2 - way * k + n2) % n2)

    def end_gather(part, n1, at1, n2, at2, slab_of, device_of):
        first, second, half1, half2, offs = gather(part, n1, at1, n2, at2, slab_of, device_of)
        for offset in range(1, NY):
            along_y(part, offset).wait_send()
        for way in (1, -1):
            for k in range(half1):
                for j in range(2):
                    if k < half1 - 1 or j == (1 - way) // 2:
                        first(k, j, way).wait_send()
            for k in range(half2):
                for t in range(n1):
                    if k < half2 - 1 or t % 2 == (1 - way) // 2:
                        second(k, t, way).wait_send()

    plan_a = (
        part_a,
        NX,
        x,
        NZ,
        z,
        lambda a, b: slab_at(a, b),
        lambda a, b: device_at(a, y, b, core),
    )
    plan_b = (
        part_b,
        NZ,
        z,
        NX,
        x,
        lambda a, b: slab_at(b, a),
        lambda a, b: device_at(b, y, a, core),
    )

    @pl.when(core == 0)
    def _():
        run_gather(*plan_a, lambda a, b: (a, b), 1)

    @pl.when(core == 1)
    def _():
        run_gather(*plan_b, lambda a, b: (b, a), 0)

    def hand_all(offset, carry):
        source = (chip + CHIPS - offset) % CHIPS
        block = rows.at[:, pl.ds(pl.multiple_of((source * 2 + core) * SLOT, SLOT), SLOT), :]
        remote(block, block, send_s.at[offset], send_r.at[offset], sibling).wait_recv()
        hand_over(offset).start()
        return carry

    lax.fori_loop(1, CHIPS, hand_all, 0)
    mask_copy.wait_recv()

    def hand_wait(offset, carry):
        hand_over(offset).wait_recv()
        return carry

    lax.fori_loop(0, CHIPS, hand_wait, 0)

    def swap_wait_a(index, carry):
        swap(part_b, index // NZ, index % NZ).wait_recv()
        return carry

    def swap_wait_b(index, carry):
        swap(part_a, 2 + index // NZ, index % NZ).wait_recv()
        return carry

    @pl.when(core == 0)
    def _():
        lax.fori_loop(0, 16, swap_wait_a, 0)

    @pl.when(core == 1)
    def _():
        lax.fori_loop(0, 16, swap_wait_b, 0)

    chip_cols = pl.ds(pl.multiple_of(chip * 128, 128), 128)

    def result(step, half):
        head = 2 * ((y + step) % NZ) + core
        target = 2 * head + half
        copy = remote(
            packed.at[step, pl.ds(half * 64, 64), :],
            out.at[:, chip_cols],
            out_s.at[2 * step + half],
            out_r.at[chip],
            (group, target),
        )
        return target, copy

    def attend(step, carry):
        head = 2 * ((y + step) % NZ) + core
        left = jnp.concatenate([part_a[head], part_a[16 + head]], axis=0)
        right = jnp.concatenate([part_b[head], part_b[16 + head]], axis=0)
        query = queries[:, pl.ds(pl.multiple_of(head * HD, HD), HD)]
        blended = []
        for clip in range(2):
            keyval = (
                nt_dot(rows[clip, :, 0:COLS_A], left) + nt_dot(rows[clip, :, COLS_A:V], right)
            ).astype(BF16)
            scores = nt_dot(query, keyval[:, :HD]) * HD ** (-0.5)
            scores = jnp.where(masks[clip] > 0.5, scores, F32(-1e30))
            raised = jnp.exp(scores - jnp.max(scores, axis=-1, keepdims=True))
            weights = (raised / jnp.sum(raised, axis=-1, keepdims=True)).astype(BF16)
            blended.append(jnp.dot(weights, keyval[:, HD:], preferred_element_type=F32))
        packed[step] = jnp.concatenate(blended, axis=0).T.astype(BF16)
        for half in range(2):
            target, copy = result(step, half)

            @pl.when(target == dev)
            def _():
                out[:, chip_cols] = packed[step, half * 64 : (half + 1) * 64, :]

            @pl.when(target != dev)
            def _():
                copy.start()

        return carry

    lax.fori_loop(0, NZ, attend, 0)

    def finish(offset, carry):
        source = (chip + CHIPS - offset) % CHIPS
        from_dev = source * 2 + (y % 2)

        @pl.when(from_dev != dev)
        def _():
            block = out.at[:, pl.ds(pl.multiple_of(source * 128, 128), 128)]
            remote(
                packed.at[0, pl.ds(0, 64), :], block, out_s.at[0], out_r.at[source], sibling
            ).wait_recv()

        return carry

    lax.fori_loop(0, CHIPS, finish, 0)

    def sent(step, carry):
        for half in range(2):
            target, copy = result(step, half)

            @pl.when(target != dev)
            def _():
                copy.wait_send()

        return carry

    lax.fori_loop(0, NZ, sent, 0)

    pair.wait_send()
    mask_copy.wait_send()

    def sent_rows(offset, carry):
        dispatch(offset).wait_send()
        return carry

    lax.fori_loop(1, CHIPS, sent_rows, 0)

    def handed(offset, carry):
        hand_over(offset).wait_send()
        return carry

    lax.fori_loop(0, CHIPS, handed, 0)

    def swapped_a(index, carry):
        swap(part_a, 2 + index // NZ, index % NZ).wait_send()
        return carry

    def swapped_b(index, carry):
        swap(part_b, index // NZ, index % NZ).wait_send()
        return carry

    @pl.when(core == 0)
    def _():
        end_gather(*plan_a)
        lax.fori_loop(0, 16, swapped_a, 0)

    @pl.when(core == 1)
    def _():
        end_gather(*plan_b)
        lax.fori_loop(0, 16, swapped_b, 0)


def per_device(
    patches,
    norm_gain,
    kv_weight,
    latent_q,
    clip_frames,
    row_owner,
    row_slot,
    slot_pos,
    latent_blocks,
):
    vmem = pl.BlockSpec(memory_space=pltpu.VMEM)
    dma = pltpu.SemaphoreType.DMA
    scratch = [
        pltpu.VMEM((32, HD, COLS_A), BF16),
        pltpu.VMEM((32, HD, COLS_B), BF16),
        pltpu.VMEM((2, CAP, V), BF16),
        pltpu.VMEM((CHIPS, 2, SLOT, V), BF16),
        pltpu.VMEM((2, 8, V), F32),
        pltpu.VMEM((2, LAT, CAP), F32),
        pltpu.VMEM((8, HD, 2 * LAT), BF16),
    ]
    scratch += [dma, dma]
    for count in (8, 16, 32, 16, 16, 16):
        scratch += [dma((count,)), dma((count,))]
    scratch += [dma, dma, dma((16,)), dma((16,))]
    return pl.pallas_call(
        kernel,
        out_shape=jax.ShapeDtypeStruct((64, 2048), BF16),
        in_specs=[vmem] * 9,
        out_specs=vmem,
        scratch_shapes=scratch,
        compiler_params=pltpu.CompilerParams(
            collective_id=0, has_side_effects=True, vmem_limit_bytes=48 * 1024 * 1024
        ),
    )(
        patches[0, 0],
        norm_gain.reshape(1, V),
        kv_weight,
        latent_q,
        clip_frames,
        row_owner[0],
        row_slot[0],
        slot_pos[0],
        latent_blocks[0, 0],
    )


def solution(mesh):
    return jax.shard_map(
        per_device,
        mesh=mesh,
        in_specs=(
            P("group", "dev", None, None),
            P(),
            P(("group", "dev"), None),
            P(),
            P("group", "dev"),
            P("group", "dev", None),
            P("group", "dev", None),
            P("group", "dev", None),
            P("group", "dev", None, None),
        ),
        out_specs=P("dev", "group"),
        check_vma=False,
    )
```

time: 912 us -> 104 us (0.11)
  waiting for transfers between devices: 807 us -> 0 us
  Pallas kernels: 0 us -> 97.7 us
  blocking collectives: 36.4 us -> 0 us
  matrix products: 17.5 us -> 0 us
  between operations: 14.2 us -> 0.69 us
  starting transfers between devices: 10.5 us -> 0 us
    all_gather x1 -> x0, waiting for transfers between devices: 777 us -> none  [project(): lax.all_gather(kv_weight, ('group', 'dev'), axis=0, tiled=True)]
    pallas_call x0 -> x1, Pallas kernels: none -> 97.7 us  [per_device(): pl.pallas_call(kernel, out_shape=jax.ShapeDtypeStruct((64, 2048), BF16),...]
    all_to_all x1 -> x0, blocking collectives: 36.4 us -> none  [per_device(): lax.all_to_all(blended, 'dev', split_axis=0, concat_axis=1, tiled=True)]
    all_to_all x1 -> x0, waiting for transfers between devices: 29.3 us -> none  [per_device(): lax.all_to_all(outbox.reshape(dev_count, slot_count, normed.shape[1]), 'd...]
    dot_general x4 -> x0, matrix products: 17.5 us -> none  [the longest x2 13.6 us: product_rows(): lax.dot_general(input_rows, weight_piece, (((1,), (1,)), ((), ())), prefe...]
    all_to_all x1 -> x0, starting transfers between devices: 10.5 us -> none  [per_device(): lax.all_to_all(outbox.reshape(dev_count, slot_count, normed.shape[1]), 'd...]
  transfers between devices with their start and end apart: 2 -> 0, of which waited for: 2 -> 0; matrix products, arithmetic and copies ran while one was open for 1% -> 0% of each run, Pallas kernels for 0% -> 0%
where the time goes in v1:
time: 104 us; the launch traced here: 103 us
  Pallas kernels  97.7 us (94%)
  local copies, waits for them, and re-layouts  4.15 us (4%)
    pallas_call x1, Pallas kernels, per_device(): pl.pallas_call(kernel, out_shape=jax.ShapeDtypeStruct((64, 2048), BF16),...  97.7 us
    unnamed x17, local copies, waits for them, and re-layouts  4.05 us

profile of v1, /device:TPU:7, one launch (start us, length us, event | category | flops | bytes accessed | tf_op | source)
XLA Modules:
  0.0 102.5 jit_solution(13251448889364006053)
XLA Ops:
  0.0 0.0 copy-start.6
  0.7 0.0 copy-done.6
  0.7 0.0 copy-start.7
  0.7 0.7 copy-done.7
  1.4 0.0 copy-start.2
  1.4 0.0 copy-start.3
  1.4 0.0 copy-start.4
  1.4 0.0 copy-start.5
  1.4 0.1 copy.10.listed
  1.5 0.6 copy-done.2
  2.1 0.0 copy-done.3
  2.1 0.0 copy-done.4
  2.1 0.0 copy-done.5
  2.1 0.0 copy-start
  2.1 1.1 %copy-done = bf16[1,1,256,1152]{3,2,1,0:T(8,128)(2,1)S(1)} copy-done((bf16[1,1,256,1152]{3,2,1,0:T(8,128)(2,1)S(1)}, bf16[1,1,256,1152]{3,2,1,0:T(8,128)(2,1)}, u32[]{:S(2)}) %copy-start) | copy-done | bytes 589848
  3.2 0.0 copy-start.1
  3.2 0.9 copy-done.1
  4.1 97.7 %shard_map.91 = bf16[64,2048]{1,0:T(8,128)(2,1)S(1)} custom-call(bf16[256,1152]{1,0:T(8,128)(2,1)S(1)} %bitcast.5, f32[1,1152]{1,0:T(1,128)S(1)} %reshape.3.gain, bf16[8,1152]{1,0:T(8,128)(2,1)S(1)} %copy-done.2, bf16[64,2048]{1,0:T(8,128)(2,1)S(1)} %copy-done.1, s32[1,1]{1,0:T(1,128)S(6)} %copy.12.frames, s32[1,256]{1,0:T(1,128)S(1)} %bitcast.7, ...), custom_call_target="tpu_custom_call" | custom-call | tf_op jit(solution)/shard_map/pallas_call | solution.py:479
  101.8 0.7 copy.13
  (1 shorter events, 0.0 us)
Async XLA Ops:
  0.0 0.7 copy-start.6
  0.7 0.7 copy-start.7
  1.4 0.7 copy-start.2
  1.4 0.7 copy-start.3
  1.4 0.7 copy-start.4
  1.4 0.7 copy-start.5
  2.1 1.1 %copy-start = (bf16[1,1,256,1152]{3,2,1,0:T(8,128)(2,1)S(1)}, bf16[1,1,256,1152]{3,2,1,0:T(8,128)(2,1)}, u32[]{:S(2)}) copy-start(bf16[1,1,256,1152]{3,2,1,0:T(8,128)(2,1)} %param.9) | copy-start | bytes 1769476
  3.2 0.9 copy-start.1

commit v2 on v1

--- a/solution.py
+++ b/solution.py
@@ -9,8 +9,8 @@
 LAT = 64
 FR_ROWS = 64
 V = 1152
-COLS_A = 640
-COLS_B = 512
+COLS_A = 512
+COLS_B = 640
 CAP = 512
 SLOT = 16
 NX, NY, NZ = 4, 8, 8
@@ -35,8 +35,19 @@
     return found + [n // 2]
 
 
+ORDER = [o + y for y in (4, 3, 5, 2, 6, 1, 7, 0) for o in (0, 8) if o + y > 0]
+FIRST, EVERY, LAG = 15, 1, 24
+EARLY_A, EARLY_B = 2, 0
+
+
 def nt_dot(left, right):
     return lax.dot_general(left, right, (((1,), (1,)), ((), ())), preferred_element_type=F32)
+
+
+def softmax(scores, mask):
+    scores = jnp.where(mask > 0.5, scores * HD ** (-0.5), F32(-1e30))
+    raised = jnp.exp(scores - jnp.max(scores, axis=-1, keepdims=True))
+    return (raised * (1.0 / jnp.sum(raised, axis=-1, keepdims=True))).astype(BF16)
 
 
 def remote(src, dst, send_sem, recv_sem, target):
@@ -167,10 +178,13 @@
         jnp.dot(onehot, normed, preferred_element_type=F32).astype(BF16).reshape(CHIPS, 2, SLOT, V)
     )
 
+    def chip_off(offset, way):
+        return (chip // 8 + offset // 8) % 2 * 8 + (chip + way * offset + 16) % 8
+
     own_rows = pl.ds(pl.multiple_of(dev * SLOT, SLOT), SLOT)
 
     def dispatch(offset):
-        there = (chip + offset) % CHIPS
+        there = chip_off(offset, 1)
         return remote(
             outbox.at[there],
             rows.at[:, own_rows, :],
@@ -180,15 +194,10 @@
         )
 
     def hand_over(offset):
-        source = (chip + CHIPS - offset) % CHIPS
+        source = chip_off(offset, -1)
         block = rows.at[:, pl.ds(pl.multiple_of((source * 2 + core) * SLOT, SLOT), SLOT), :]
         return remote(block, block, hand_s.at[offset], hand_r.at[offset], sibling)
 
-    def start_dispatch(offset, carry):
-        dispatch(offset).start()
-        return carry
-
-    lax.fori_loop(1, CHIPS, start_dispatch, 0)
     rows[:, own_rows, :] = outbox[chip]
     hand_over(0).start()
 
@@ -227,7 +236,79 @@
         block = part.at[slab_at(sx, sz)]
         return remote(block, block, swap_s.at[index], swap_r.at[index], sibling)
 
-    def run_gather(part, n1, at1, n2, at2, slab_of, device_of, xz_of, other):
+    def hand_one(offset):
+        dispatch(offset).wait_recv()
+        hand_over(offset).start()
+
+    chip_cols = pl.ds(pl.multiple_of(chip * 128, 128), 128)
+
+    def head_of(step):
+        return 2 * ((z + NZ + (step + 1) // 2 * (2 * (step % 2) - 1)) % NZ) + core
+
+    def result(step, half):
+        target = 2 * head_of(step) + half
+        copy = remote(
+            packed.at[step, pl.ds(half * 64, 64), :],
+            out.at[:, chip_cols],
+            out_s.at[2 * step + half],
+            out_r.at[chip],
+            (group, target),
+        )
+        return target, copy
+
+    def attend(lowest, count):
+        heads = [head_of(lowest + i) for i in range(count)]
+        blocks, scored = [], []
+        for head in heads:
+            both = jnp.concatenate(
+                [
+                    jnp.concatenate([part_a[head], part_a[16 + head]], axis=0),
+                    jnp.concatenate([part_b[head], part_b[16 + head]], axis=0),
+                ],
+                axis=1,
+            )
+            blocks.append([nt_dot(both, rows[clip]).astype(BF16) for clip in range(2)])
+        for i, head in enumerate(heads):
+            query = queries[:, pl.ds(pl.multiple_of(head * HD, HD), HD)]
+            scored.append(
+                [jnp.dot(query, part[:HD], preferred_element_type=F32) for part in blocks[i]]
+            )
+        weights = [[softmax(one[clip], masks[clip]) for clip in range(2)] for one in scored]
+        for i in range(count):
+            packed[lowest + i] = jnp.concatenate(
+                [nt_dot(blocks[i][clip][HD:], weights[i][clip]) for clip in range(2)], axis=1
+            ).astype(BF16)
+        for i in range(count):
+            for half in range(2):
+                send_result(lowest + i, half)
+
+    def send_result(step, half):
+        target, copy = result(step, half)
+
+        @pl.when(target == dev)
+        def _():
+            out[:, chip_cols] = packed[step, half * 64 : (half + 1) * 64, :]
+
+        @pl.when(target != dev)
+        def _():
+            copy.start()
+
+    def attend_pairs(other_part, low, high):
+        def pair_of_heads(u, carry):
+            for i in range(2):
+                place = head_of(2 * u + i) // 2
+                for half in range(2):
+                    swap(other_part, 2 * core + half, place).wait_recv()
+            attend(2 * u, 2)
+            return carry
+
+        lax.fori_loop(low, high, pair_of_heads, 0)
+
+    def hand_wait(offset, carry):
+        hand_over(offset).wait_recv()
+        return carry
+
+    def run_gather(part, n1, at1, n2, at2, slab_of, device_of, xz_of, other, other_part, early):
         first, second, half1, half2, offs = gather(part, n1, at1, n2, at2, slab_of, device_of)
 
         def landed(t, place2):
@@ -241,6 +322,17 @@
             second(0, t, 1).start()
             second(0, t, -1).start()
             landed(t, at2)
+
+        state = [0, 0, 0]
+
+        def tick():
+            state[0] += 1
+            while state[1] < len(ORDER) and state[1] < FIRST + (state[0] - 1) / EVERY:
+                dispatch(ORDER[state[1]]).start()
+                state[1] += 1
+            while state[2] < len(ORDER) and state[2] < FIRST + (state[0] - 1 - LAG) / EVERY:
+                hand_one(ORDER[state[2]])
+                state[2] += 1
 
         for offset in range(1, NY):
             along_y(part, offset).wait_recv()
@@ -248,6 +340,7 @@
             for way in (1, -1):
                 first(0, j, way).start()
         complete(0)
+        tick()
         for k in range(1, half1 + 1):
             for way in (-1, 1):
                 for j in range(2):
@@ -259,8 +352,18 @@
                         first(k, j, way).start()
                 if k < half1:
                     complete(2 * k if way == 1 else 2 * k - 1)
+                    tick()
         complete(n1 - 1)
+        tick()
         for k in range(1, half2 + 1):
+            if k == half2:
+                for offset in ORDER[state[1] :]:
+                    dispatch(offset).start()
+                for offset in ORDER[state[2] :]:
+                    hand_one(offset)
+                mask_copy.wait_recv()
+                lax.fori_loop(0, CHIPS, hand_wait, 0)
+                attend_pairs(other_part, 0, early)
             for t in range(n1):
                 for way in (1, -1):
                     chosen = t % 2 == (1 - way) // 2
@@ -270,6 +373,9 @@
                     if k < half2 - 1 or (k == half2 - 1 and chosen):
                         second(k, t, way).start()
                     landed(t, (at2 - way * k + n2) % n2)
+                    if k < half2:
+                        tick()
+        attend_pairs(other_part, early, NZ // 2)
 
     def end_gather(part, n1, at1, n2, at2, slab_of, device_of):
         first, second, half1, half2, offs = gather(part, n1, at1, n2, at2, slab_of, device_of)
@@ -306,88 +412,11 @@
 
     @pl.when(core == 0)
     def _():
-        run_gather(*plan_a, lambda a, b: (a, b), 1)
+        run_gather(*plan_a, lambda a, b: (a, b), 1, part_b, EARLY_A)
 
     @pl.when(core == 1)
     def _():
-        run_gather(*plan_b, lambda a, b: (b, a), 0)
-
-    def hand_all(offset, carry):
-        source = (chip + CHIPS - offset) % CHIPS
-        block = rows.at[:, pl.ds(pl.multiple_of((source * 2 + core) * SLOT, SLOT), SLOT), :]
-        remote(block, block, send_s.at[offset], send_r.at[offset], sibling).wait_recv()
-        hand_over(offset).start()
-        return carry
-
-    lax.fori_loop(1, CHIPS, hand_all, 0)
-    mask_copy.wait_recv()
-
-    def hand_wait(offset, carry):
-        hand_over(offset).wait_recv()
-        return carry
-
-    lax.fori_loop(0, CHIPS, hand_wait, 0)
-
-    def swap_wait_a(index, carry):
-        swap(part_b, index // NZ, index % NZ).wait_recv()
-        return carry
-
-    def swap_wait_b(index, carry):
-        swap(part_a, 2 + index // NZ, index % NZ).wait_recv()
-        return carry
-
-    @pl.when(core == 0)
-    def _():
-        lax.fori_loop(0, 16, swap_wait_a, 0)
-
-    @pl.when(core == 1)
-    def _():
-        lax.fori_loop(0, 16, swap_wait_b, 0)
-
-    chip_cols = pl.ds(pl.multiple_of(chip * 128, 128), 128)
-
-    def result(step, half):
-        head = 2 * ((y + step) % NZ) + core
-        target = 2 * head + half
-        copy = remote(
-            packed.at[step, pl.ds(half * 64, 64), :],
-            out.at[:, chip_cols],
-            out_s.at[2 * step + half],
-            out_r.at[chip],
-            (group, target),
-        )
-        return target, copy
-
-    def attend(step, carry):
-        head = 2 * ((y + step) % NZ) + core
-        left = jnp.concatenate([part_a[head], part_a[16 + head]], axis=0)
-        right = jnp.concatenate([part_b[head], part_b[16 + head]], axis=0)
-        query = queries[:, pl.ds(pl.multiple_of(head * HD, HD), HD)]
-        blended = []
-        for clip in range(2):
-            keyval = (
-                nt_dot(rows[clip, :, 0:COLS_A], left) + nt_dot(rows[clip, :, COLS_A:V], right)
-            ).astype(BF16)
-            scores = nt_dot(query, keyval[:, :HD]) * HD ** (-0.5)
-            scores = jnp.where(masks[clip] > 0.5, scores, F32(-1e30))
-            raised = jnp.exp(scores - jnp.max(scores, axis=-1, keepdims=True))
-            weights = (raised / jnp.sum(raised, axis=-1, keepdims=True)).astype(BF16)
-            blended.append(jnp.dot(weights, keyval[:, HD:], preferred_element_type=F32))
-        packed[step] = jnp.concatenate(blended, axis=0).T.astype(BF16)
-        for half in range(2):
-            target, copy = result(step, half)
-
-            @pl.when(target == dev)
-            def _():
-                out[:, chip_cols] = packed[step, half * 64 : (half + 1) * 64, :]
-
-            @pl.when(target != dev)
-            def _():
-                copy.start()
-
-        return carry
-
-    lax.fori_loop(0, NZ, attend, 0)
+        run_gather(*plan_b, lambda a, b: (b, a), 0, part_a, EARLY_B)
 
     def finish(offset, carry):
         source = (chip + CHIPS - offset) % CHIPS

time: 104 us -> 79.9 us (0.77)
  the two profiles are of different devices: /device:TPU:7 before, /device:TPU:13 now
where the time goes in v2:
time: 79.9 us; the launch traced here: 79.6 us
  Pallas kernels  74.7 us (93%)
  local copies, waits for them, and re-layouts  4.15 us (5%)
    pallas_call x1, Pallas kernels, per_device(): pl.pallas_call(kernel, out_shape=jax.ShapeDtypeStruct((64, 2048), BF16),...  74.7 us
    unnamed x17, local copies, waits for them, and re-layouts  4.05 us

profile of v2, /device:TPU:13, one launch (start us, length us, event | category | flops | bytes accessed | tf_op | source)
XLA Modules:
  0.0 79.6 jit_solution(16311611447425176457)
XLA Ops:
  0.0 0.0 copy-start.6
  0.7 0.0 copy-done.6
  0.7 0.0 copy-start.7
  0.7 0.7 copy-done.7
  1.4 0.0 copy-start.2
  1.4 0.0 copy-start.3
  1.4 0.0 copy-start.4
  1.4 0.0 copy-start.5
  1.4 0.1 copy.10.listed
  1.5 0.6 copy-done.2
  2.1 0.0 copy-done.3
  2.1 0.0 copy-done.4
  2.1 0.0 copy-done.5
  2.1 0.0 copy-start
  2.1 1.1 %copy-done = bf16[1,1,256,1152]{3,2,1,0:T(8,128)(2,1)S(1)} copy-done((bf16[1,1,256,1152]{3,2,1,0:T(8,128)(2,1)S(1)}, bf16[1,1,256,1152]{3,2,1,0:T(8,128)(2,1)}, u32[]{:S(2)}) %copy-start) | copy-done | bytes 589848
  3.2 0.0 copy-start.1
  3.2 0.9 %copy-done.1 = bf16[64,2048]{1,0:T(8,128)(2,1)S(1)} copy-done((bf16[64,2048]{1,0:T(8,128)(2,1)S(1)}, bf16[64,2048]{1,0:T(8,128)(2,1)}, u32[]{:S(2)}) %copy-start.1) | copy-done | bytes 262168
  4.1 74.7 %shard_map.91 = bf16[64,2048]{1,0:T(8,128)(2,1)S(1)} custom-call(bf16[256,1152]{1,0:T(8,128)(2,1)S(1)} %bitcast.5, f32[1,1152]{1,0:T(1,128)S(1)} %reshape.3.gain, bf16[8,1152]{1,0:T(8,128)(2,1)S(1)} %copy-done.2, bf16[64,2048]{1,0:T(8,128)(2,1)S(1)} %copy-done.1, s32[1,1]{1,0:T(1,128)S(6)} %copy.12.frames, s32[1,256]{1,0:T(1,128)S(1)} %bitcast.7, ...), custom_call_target="tpu_custom_call" | custom-call | tf_op jit(solution)/shard_map/pallas_call | solution.py:508
  78.9 0.7 copy.13
  (1 shorter events, 0.0 us)
Async XLA Ops:
  0.0 0.7 copy-start.6
  0.7 0.7 copy-start.7
  1.4 0.7 copy-start.2
  1.4 0.7 copy-start.3
  1.4 0.7 copy-start.4
  1.4 0.7 copy-start.5
  2.1 1.1 %copy-start = (bf16[1,1,256,1152]{3,2,1,0:T(8,128)(2,1)S(1)}, bf16[1,1,256,1152]{3,2,1,0:T(8,128)(2,1)}, u32[]{:S(2)}) copy-start(bf16[1,1,256,1152]{3,2,1,0:T(8,128)(2,1)} %param.9) | copy-start | bytes 1769476
  3.2 0.9 %copy-start.1 = (bf16[64,2048]{1,0:T(8,128)(2,1)S(1)}, bf16[64,2048]{1,0:T(8,128)(2,1)}, u32[]{:S(2)}) copy-start(bf16[64,2048]{1,0:T(8,128)(2,1)} %queries.1) | copy-start | bytes 786436

commit v3 on v0

v3 whole, which is shorter than its diff:
```python
import jax
import jax.numpy as jnp
from jax import lax
from jax.experimental import pallas as pl
from jax.experimental.pallas import tpu as pltpu
from jax.sharding import PartitionSpec as P

HD = 128
LAT = 64
FR_ROWS = 64
V = 1152
COLS_A = 640
COLS_B = 512
CAP = 512
SLOT = 16
NX, NY, NZ = 4, 8, 8
MESH = pl.DeviceIdType.MESH
F32 = jnp.float32
BF16 = jnp.bfloat16


def device_at(x, y, z, core):
    return ((x % 2) * NZ + z, (x // 2) * 2 * NY + y * 2 + core)


def slab_at(x, z):
    return ((x % 2) * NZ + z) * 2 + x // 2


ORDER = (1, 7, 2, 6, 3, 5, 4)
ROWS_AT = {
    0: ((1, 7), ()),
    2: ((), (0,)),
    3: ((2, 6), ()),
    5: ((), (1, 7)),
    7: ((3, 5), ()),
    8: ((), (2, 6)),
    11: ((4,), ()),
    12: ((), (3, 5)),
}
FIRST = (1, 7)


def nt_dot(left, right):
    return lax.dot_general(left, right, (((1,), (1,)), ((), ())), preferred_element_type=F32)


def softmax(scores, mask):
    scores = jnp.where(mask > 0.5, scores * HD ** (-0.5), F32(-1e30))
    raised = jnp.exp(scores - jnp.max(scores, axis=-1, keepdims=True))
    return (raised * (1.0 / jnp.sum(raised, axis=-1, keepdims=True))).astype(BF16)


def remote(src, dst, send_sem, recv_sem, target):
    return pltpu.make_async_remote_copy(
        src_ref=src,
        dst_ref=dst,
        send_sem=send_sem,
        recv_sem=recv_sem,
        device_id=target,
        device_id_type=MESH,
    )


def kernel(
    patches_far,
    gain,
    weight,
    queries_far,
    frames,
    owner,
    slot,
    places,
    listed,
    out,
    part_a,
    part_b,
    rows,
    outbox,
    wide,
    meta,
    masks,
    packed,
    patches,
    queries,
    near_s,
    pair_s,
    pair_r,
    ring_y_s,
    ring_y_r,
    first_s,
    first_r,
    second_s,
    second_r,
    swap_s,
    swap_r,
    send_s,
    send_r,
    cross_s,
    cross_r,
    hand_s,
    hand_r,
    meta_s,
    meta_r,
    out_s,
    out_r,
):
    group = lax.axis_index("group")
    dev = lax.axis_index("dev")
    x_lo, z = group // NZ, group % NZ
    x_hi, in_line = dev // (2 * NY), dev % (2 * NY)
    y, core = in_line // 2, in_line % 2
    x = x_hi * 2 + x_lo
    sibling = (group, x_hi * 2 * NY + y * 2 + 1 - core)
    partner = (group, (1 - x_hi) * 2 * NY + y * 2 + core)
    partner_sibling = (group, (1 - x_hi) * 2 * NY + y * 2 + 1 - core)
    beside = ((1 - x_lo) * NZ + z, dev)

    near = [
        pltpu.make_async_copy(patches_far, patches, near_s.at[0]),
        pltpu.make_async_copy(queries_far, queries, near_s.at[1]),
    ]
    for copy in near:
        copy.start()

    barrier = pltpu.get_barrier_semaphore()

    def greet(offset, carry):
        pl.semaphore_signal(
            barrier, inc=1, device_id=(group, (dev + offset) % 32), device_id_type=MESH
        )
        return carry

    lax.fori_loop(1, 32, greet, 0)
    for target in (
        device_at(x, y, (z + 1) % NZ, core),
        device_at(x, y, (z + NZ - 1) % NZ, core),
        beside,
    ):
        pl.semaphore_signal(barrier, inc=1, device_id=target, device_id_type=MESH)
    own_rows = pl.ds(pl.multiple_of(dev * SLOT, SLOT), SLOT)

    def rows_of(x_hi_from, offset):
        source = x_hi_from * 2 * NY + (y + NY - offset) % NY * 2 + core
        return rows.at[:, :, pl.ds(pl.multiple_of(source * SLOT, SLOT), SLOT), :]

    def dispatch(offset):
        there = (y + offset) % NY
        return remote(
            outbox.at[:, there],
            rows.at[:, :, own_rows, :],
            send_s.at[offset],
            send_r.at[offset],
            (group, x_hi * 2 * NY + there * 2 + core),
        )

    def cross(offset):
        block = rows_of(x_hi, offset)
        return remote(block, block, cross_s.at[offset], cross_r.at[offset], partner)

    def hand_over(far, offset):
        block = rows_of(1 - x_hi if far else x_hi, offset)
        index = far * NY + offset
        return remote(block, block, hand_s.at[index], hand_r.at[index], sibling)

    near[0].wait()
    widened = patches[...].astype(F32)
    inverse_rms = lax.rsqrt(jnp.sum(widened * widened, axis=-1, keepdims=True) * (1.0 / V) + 1e-06)
    normed = (widened * inverse_rms * gain[...].reshape(1, V)).astype(BF16)
    target_slot = owner[...] * SLOT + slot[...]
    onehot = (
        lax.broadcasted_iota(jnp.int32, (CAP, target_slot.shape[1]), 0) == target_slot
    ).astype(F32).astype(BF16)
    outbox[...] = (
        jnp.dot(onehot, normed, preferred_element_type=F32).astype(BF16).reshape(2, NY, 2, SLOT, V)
    )
    rows[:, :, own_rows, :] = outbox[:, y]
    pl.semaphore_wait(barrier, 34)

    cross(0).start()
    hand_over(0, 0).start()
    for offset in FIRST:
        dispatch(offset).start()

    wide[core] = weight[...].astype(F32)
    pair = remote(wide.at[core], wide.at[core], pair_s, pair_r, sibling)
    pair.start()

    position = places[...]
    marks = listed[...]
    block_of = lax.broadcasted_iota(jnp.int32, (8, CAP), 0)
    in_block = (block_of == position // (2 * FR_ROWS)) & (position < frames[...] * FR_ROWS)
    named = lax.broadcasted_iota(jnp.int32, (8, LAT), 0)
    named = (named == marks[0:1, :]) | (named == marks[1:2, :])
    meta[x_hi, core, :, 0:CAP] = jnp.where(in_block, F32(1.0), F32(0.0))
    meta[x_hi, core, :, CAP : CAP + LAT] = jnp.where(named, F32(1.0), F32(0.0))
    own_meta = meta.at[x_hi, core]
    meta_copies = [
        remote(own_meta, own_meta, meta_s.at[i], meta_r.at[i], target)
        for i, target in enumerate((sibling, partner, partner_sibling))
    ]
    for copy in meta_copies:
        copy.start()
    pair.wait_recv()

    chip_rows = pl.ds(pl.multiple_of(y * 16, 16), 16)
    mine = slab_at(x, z)

    def spread(part, low, high):
        both = jnp.concatenate([wide[0, :, low:high], wide[1, :, low:high]], axis=0)
        part[mine, chip_rows, :] = both.astype(BF16)
        for offset in range(1, NY):
            along_y(part, offset).start()

    def along_y(part, offset):
        block = part.at[mine, chip_rows, :]
        return remote(
            block,
            block,
            ring_y_s.at[offset],
            ring_y_r.at[offset],
            device_at(x, (y + offset) % NY, z, core),
        )

    @pl.when(core == 0)
    def _():
        spread(part_a, 0, COLS_A)

    @pl.when(core == 1)
    def _():
        spread(part_b, COLS_A, V)

    for offset in ORDER:
        if offset not in FIRST:
            dispatch(offset).start()
    near[1].wait()

    def pair_slab(t, place):
        return slab_at(x_hi * 2 + (x_lo + t) % 2, place)

    def first(part):
        block = part.at[mine]
        return remote(block, block, first_s, first_r, beside)

    def second(part, k, t, way):
        block = part.at[pair_slab(t, (z - way * k + NZ) % NZ)]
        index = ((way + 1) // 2 * (NZ // 2) + k) * 2 + t
        return remote(
            block,
            block,
            second_s.at[index],
            second_r.at[index],
            device_at(x, y, (z + way + NZ) % NZ, core),
        )

    def swap(part, t, place):
        block = part.at[pair_slab(t, place)]
        index = (x_lo + t) % 2 * NZ + place
        return remote(block, block, swap_s.at[index], swap_r.at[index], sibling)

    def place_of(step):
        return (step + y) % (NZ // 2) * 2 + core

    def head_of(step):
        return 2 * place_of(step) + x_hi

    def clip_cols(side, line):
        return pl.ds(pl.multiple_of(side * 1024 + line * 128, 128), 128)

    def result(step, half, side):
        target = 2 * head_of(step) + half
        copy = remote(
            packed.at[step, side, pl.ds(half * 64, 64), :],
            out.at[:, clip_cols(side, y)],
            out_s.at[(2 * step + half) * 2 + side],
            out_r.at[side * NY + y],
            (group, target),
        )
        return target, copy

    def attend(step):
        head = head_of(step)
        both = jnp.concatenate(
            [
                jnp.concatenate([part_a[head], part_a[16 + head]], axis=0),
                jnp.concatenate([part_b[head], part_b[16 + head]], axis=0),
            ],
            axis=1,
        )
        query = queries[:, pl.ds(pl.multiple_of(head * HD, HD), HD)]
        clips = [(side, i) for side in range(2) for i in range(2)]
        blocks = [nt_dot(both, rows[side, i]).astype(BF16) for side, i in clips]
        scored = [jnp.dot(query, part[:HD], preferred_element_type=F32) for part in blocks]
        weights = [softmax(scored[n], masks[side, i]) for n, (side, i) in enumerate(clips)]
        blended = [nt_dot(blocks[n][HD:], weights[n]) for n in range(4)]
        for side in range(2):
            packed[step, side] = jnp.concatenate(
                blended[2 * side : 2 * side + 2], axis=1
            ).astype(BF16)
        for half in range(2):
            for side in range(2):
                send_result(step, half, side)

    def send_result(step, half, side):
        target, copy = result(step, half, side)

        @pl.when(target == dev)
        def _():
            out[:, clip_cols(side, y)] = packed[step, side, half * 64 : (half + 1) * 64, :]

        @pl.when(target != dev)
        def _():
            copy.start()

    def attend_all(other_part, low, high):
        def one_head(step, carry):
            for t in range(2):
                swap(other_part, t, place_of(step)).wait_recv()
            attend(step)
            return carry

        lax.fori_loop(low, high, one_head, 0)

    def hand_wait(index, carry):
        block = rows_of(x_hi, 0)
        remote(block, block, hand_s.at[index], hand_r.at[index], sibling).wait_recv()
        return carry

    def arrived(offset):
        dispatch(offset).wait_recv()
        cross(offset).start()
        hand_over(0, offset).start()

    def crossed(offset):
        cross(offset).wait_recv()
        hand_over(1, offset).start()

    def run_gather(part, other_part, other):
        state = [0, [], []]

        def move_rows(near_rows, far_rows):
            for offset in near_rows:
                arrived(offset)
            for offset in far_rows:
                crossed(offset)
            for i, new in enumerate((near_rows, far_rows)):
                state[i + 1] += new

        def tick():
            move_rows(*ROWS_AT.get(state[0], ((), ())))
            state[0] += 1

        def landed(t, place):
            @pl.when(place % 2 == other)
            def _():
                swap(part, t, place).start()

        for offset in range(1, NY):
            along_y(part, offset).wait_recv()
        first(part).start()
        for t in range(2):
            if t == 1:
                first(part).wait_recv()
            for way in (1, -1):
                second(part, 0, t, way).start()
            landed(t, z)
            if t == 0:
                tick()
        tick()
        for k in range(1, NZ // 2 + 1):
            for t in range(2):
                for way in (1, -1):
                    chosen = t == (1 - way) // 2
                    if k == NZ // 2 and not chosen:
                        continue
                    second(part, k - 1, t, way).wait_recv()
                    if k < NZ // 2 - 1 or (k == NZ // 2 - 1 and chosen):
                        second(part, k, t, way).start()
                    landed(t, (z - way * k + NZ) % NZ)
                    tick()
        for copy in meta_copies:
            copy.wait_recv()
        for side in range(2):
            for i in range(2):
                masks[side, i] = lax.dot_general(
                    meta[side, i, :, CAP : CAP + LAT],
                    meta[side, i, :, 0:CAP],
                    (((0,), (0,)), ((), ())),
                    preferred_element_type=F32,
                )
        left = [
            tuple(o for o in (0,) + ORDER if o not in done and (i == 1 or o))
            for i, done in enumerate(state[1:])
        ]
        move_rows(*left)
        lax.fori_loop(0, 2 * NY, hand_wait, 0)
        attend_all(other_part, 0, NZ // 2)

    @pl.when(core == 0)
    def _():
        run_gather(part_a, part_b, 1)

    @pl.when(core == 1)
    def _():
        run_gather(part_b, part_a, 0)

    def finish(line, carry):
        source = (y % 2) * 2 * NY + line * 2 + (y // 2) % 2

        @pl.when(source != dev)
        def _():
            for side in range(2):
                remote(
                    packed.at[0, side, pl.ds(0, 64), :],
                    out.at[:, clip_cols(side, line)],
                    out_s.at[0],
                    out_r.at[side * NY + line],
                    sibling,
                ).wait_recv()

        return carry

    lax.fori_loop(0, NY, finish, 0)

    def sent(step, carry):
        for half in range(2):
            for side in range(2):
                target, copy = result(step, half, side)

                @pl.when(target != dev)
                def _():
                    copy.wait_send()

        return carry

    lax.fori_loop(0, NZ // 2, sent, 0)

    pair.wait_send()
    for copy in meta_copies:
        copy.wait_send()

    def sent_rows(offset, carry):
        @pl.when(offset > 0)
        def _():
            dispatch(offset).wait_send()

        cross(offset).wait_send()
        for far in range(2):
            hand_over(far, offset).wait_send()
        return carry

    lax.fori_loop(0, NY, sent_rows, 0)

    def end_gather(part, other):
        for offset in range(1, NY):
            along_y(part, offset).wait_send()
        first(part).wait_send()
        for way in (1, -1):
            for k in range(NZ // 2):
                for t in range(2):
                    if k < NZ // 2 - 1 or t == (1 - way) // 2:
                        second(part, k, t, way).wait_send()
        for t in range(2):
            for place in range(other, NZ, 2):
                swap(part, t, place).wait_send()

    @pl.when(core == 0)
    def _():
        end_gather(part_a, 1)

    @pl.when(core == 1)
    def _():
        end_gather(part_b, 0)


def per_device(
    patches,
    norm_gain,
    kv_weight,
    latent_q,
    clip_frames,
    row_owner,
    row_slot,
    slot_pos,
    latent_blocks,
):
    vmem = pl.BlockSpec(memory_space=pltpu.VMEM)
    far = pl.BlockSpec(memory_space=pltpu.HBM)
    dma = pltpu.SemaphoreType.DMA
    scratch = [
        pltpu.VMEM((32, HD, COLS_A), BF16),
        pltpu.VMEM((32, HD, COLS_B), BF16),
        pltpu.VMEM((2, 2, CAP, V), BF16),
        pltpu.VMEM((2, NY, 2, SLOT, V), BF16),
        pltpu.VMEM((2, 8, V), F32),
        pltpu.VMEM((2, 2, 8, CAP + HD), F32),
        pltpu.VMEM((2, 2, LAT, CAP), F32),
        pltpu.VMEM((4, 2, HD, 2 * LAT), BF16),
        pltpu.VMEM((256, V), BF16),
        pltpu.VMEM((LAT, 2048), BF16),
        dma((2,)),
        dma,
        dma,
        dma((8,)),
        dma((8,)),
        dma,
        dma,
    ]
    for count in (16, 16, 8, 8, 16, 3, 16):
        scratch += [dma((count,)), dma((count,))]
    return pl.pallas_call(
        kernel,
        out_shape=jax.ShapeDtypeStruct((64, 2048), BF16),
        in_specs=[far, vmem, vmem, far] + [vmem] * 5,
        out_specs=vmem,
        scratch_shapes=scratch,
        compiler_params=pltpu.CompilerParams(
            collective_id=0, has_side_effects=True, vmem_limit_bytes=63 * 1024 * 1024
        ),
    )(
        patches[0, 0],
        norm_gain,
        kv_weight,
        latent_q,
        clip_frames,
        row_owner[0],
        row_slot[0],
        slot_pos[0],
        latent_blocks[0, 0].T,
    )


def solution(mesh):
    return jax.shard_map(
        per_device,
        mesh=mesh,
        in_specs=(
            P("group", "dev", None, None),
            P(),
            P(("group", "dev"), None),
            P(),
            P("group", "dev"),
            P("group", "dev", None),
            P("group", "dev", None),
            P("group", "dev", None),
            P("group", "dev", None, None),
        ),
        out_specs=P("dev", "group"),
        check_vma=False,
    )
```

time: 912 us -> 73.5 us (0.08)
  waiting for transfers between devices: 807 us -> 0 us
  Pallas kernels: 0 us -> 71 us
  blocking collectives: 36.4 us -> 0 us
  matrix products: 17.5 us -> 0 us
  between operations: 14.2 us -> 0.66 us
  starting transfers between devices: 10.5 us -> 0 us
  local copies, waits for them, and re-layouts: 12.1 us -> 1.67 us
    all_gather x1 -> x0, waiting for transfers between devices: 777 us -> none  [project(): lax.all_gather(kv_weight, ('group', 'dev'), axis=0, tiled=True)]
    pallas_call x0 -> x1, Pallas kernels: none -> 71 us  [per_device(): pl.pallas_call(kernel, out_shape=jax.ShapeDtypeStruct((64, 2048), BF16),...]
    all_to_all x1 -> x0, blocking collectives: 36.4 us -> none  [per_device(): lax.all_to_all(blended, 'dev', split_axis=0, concat_axis=1, tiled=True)]
    all_to_all x1 -> x0, waiting for transfers between devices: 29.3 us -> none  [per_device(): lax.all_to_all(outbox.reshape(dev_count, slot_count, normed.shape[1]), 'd...]
    dot_general x4 -> x0, matrix products: 17.5 us -> none  [the longest x2 13.6 us: product_rows(): lax.dot_general(input_rows, weight_piece, (((1,), (1,)), ((), ())), prefe...]
    all_to_all x1 -> x0, starting transfers between devices: 10.5 us -> none  [per_device(): lax.all_to_all(outbox.reshape(dev_count, slot_count, normed.shape[1]), 'd...]
  transfers between devices with their start and end apart: 2 -> 0, of which waited for: 2 -> 0; matrix products, arithmetic and copies ran while one was open for 1% -> 0% of each run, Pallas kernels for 0% -> 0%
where the time goes in v3:
time: 73.5 us; the launch traced here: 73.3 us
  Pallas kernels  71 us (97%)
  local copies, waits for them, and re-layouts  1.67 us (2%)
    pallas_call x1, Pallas kernels, per_device(): pl.pallas_call(kernel, out_shape=jax.ShapeDtypeStruct((64, 2048), BF16),...  71 us
    unnamed x1, local copies, waits for them, and re-layouts  1.67 us

profile of v3, /device:TPU:7, one launch (start us, length us, event | category | flops | bytes accessed | tf_op | source)
XLA Modules:
  0.0 73.3 jit_solution(4664964252933200588)
XLA Ops:
  0.7 71.0 %shard_map.91 = bf16[64,2048]{1,0:T(8,128)(2,1)} custom-call(bf16[256,1152]{1,0:T(8,128)(2,1)} %bitcast.7, f32[1152]{0:T(1024)} %gain.1, bf16[8,1152]{1,0:T(8,128)(2,1)} %weight.1, bf16[64,2048]{1,0:T(8,128)(2,1)} %queries_far.1, s32[1,1]{1,0:T(1,128)S(6)} %copy.11.frames, s32[1,256]{1,0:T(1,128)} %bitcast.9, s32[1,256]{1,0:T(1,128)} %bitcast.10, ...), custom_call_target="tpu_custom_call" | custom-call | tf_op jit(solution)/shard_map/pallas_call | solution.py:511
  71.7 1.7 %copy.12 = bf16[64,2048]{1,0:T(8,128)(2,1)} copy(bf16[64,2048]{1,0:T(8,128)(2,1)} %shard_map.91) | data formatting | bytes 524288

commit v4 on v3

--- a/solution.py
+++ b/solution.py
@@ -35,7 +35,7 @@
     5: ((), (1, 7)),
     7: ((3, 5), ()),
     8: ((), (2, 6)),
-    11: ((4,), ()),
+    10: ((4,), ()),
     12: ((), (3, 5)),
 }
 FIRST = (1, 7)

time: 73.5 us -> 73.5 us (level)
  no operation moved by 1% of the time
where the time goes in v4:
time: 73.5 us; the launch traced here: 73.3 us
  Pallas kernels  71 us (97%)
  local copies, waits for them, and re-layouts  1.67 us (2%)
    pallas_call x1, Pallas kernels, per_device(): pl.pallas_call(kernel, out_shape=jax.ShapeDtypeStruct((64, 2048), BF16),...  71 us
    unnamed x1, local copies, waits for them, and re-layouts  1.67 us

profile of v4, /device:TPU:7, one launch (start us, length us, event | category | flops | bytes accessed | tf_op | source)
XLA Modules:
  0.0 73.3 jit_solution(10900007166873420021)
XLA Ops:
  0.7 71.0 %shard_map.91 = bf16[64,2048]{1,0:T(8,128)(2,1)} custom-call(bf16[256,1152]{1,0:T(8,128)(2,1)} %bitcast.7, f32[1152]{0:T(1024)} %gain.1, bf16[8,1152]{1,0:T(8,128)(2,1)} %weight.1, bf16[64,2048]{1,0:T(8,128)(2,1)} %queries_far.1, s32[1,1]{1,0:T(1,128)S(6)} %copy.11.frames, s32[1,256]{1,0:T(1,128)} %bitcast.9, s32[1,256]{1,0:T(1,128)} %bitcast.10, ...), custom_call_target="tpu_custom_call" | custom-call | tf_op jit(solution)/shard_map/pallas_call | solution.py:511
  71.6 1.7 %copy.12 = bf16[64,2048]{1,0:T(8,128)(2,1)} copy(bf16[64,2048]{1,0:T(8,128)(2,1)} %shard_map.91) | data formatting | bytes 524288
